TPU v7x, 256 devices: a whole 4x4x8 slice. The times are simulated.
256 devices in a mesh: tm: 4 (over y), space: 64 (over z, x, core).
Axes of the slice: x: 4, y: 4, z: 8, core: 2. Of those that a mesh axis runs over, the one named last changes fastest.
Arguments:
- latents: bfloat16 [4, 64, 8, 40, 384], P('tm', 'space'), may hold values from -8 to 8
- gain_first: float32 [384], replicated, may hold values from 0.5 to 2
- shift_first: float32 [384], replicated, may hold values from -3 to 3
- kernel_first: bfloat16 [3, 3, 3, 384, 384], P(None, None, None, 'space', 'tm'), may hold values from -0.0625 to 0.0625
- bias_first: float32 [384], replicated, may hold values from -3 to 3
- gain_second: float32 [384], replicated, may hold values from 0.5 to 2
- shift_second: float32 [384], replicated, may hold values from -3 to 3
- kernel_second: bfloat16 [3, 3, 3, 384, 384], P(None, None, None, 'space', 'tm'), may hold values from -0.0625 to 0.0625
- bias_second: float32 [384], replicated, may hold values from -3 to 3
Outputs:
- decoded: bfloat16 [4, 64, 8, 40, 384], P('tm', 'space')
All inputs are finite; a program needn't handle non-finite values.
Results may differ from a plain program's by a relative error of at most 0.0085.
Values may be sent and summed in bfloat16 or wider, within the bound.
No kernel may reach another device: no remote copies, remote signals or barrier semaphores. Data moves between devices by JAX's collectives and lax.ppermute only.
A program may use at most 128 MiB of HBM per device.

v0:
```python
import jax
import jax.numpy as jnp
from jax import lax
from jax.sharding import PartitionSpec as P

GROUPS = 32
GX = 8
EPS = 1e-06


def shifted(value, axis, steps):
    count = lax.axis_size(axis)
    initial, last = (max(0, -steps), min(count, count - steps))
    return lax.ppermute(value, axis, [(source, source + steps) for source in range(initial, last)])


def spatial_halo(tile):
    column = lax.axis_index("space") % GX
    from_west = shifted(tile[:, -1:, :], "space", 1)
    from_east = shifted(tile[:, :1, :], "space", -1)
    from_west = jnp.where(column > 0, from_west, jnp.zeros_like(from_west))
    from_east = jnp.where(column < GX - 1, from_east, jnp.zeros_like(from_east))
    widened = jnp.concatenate([from_west, tile, from_east], axis=1)
    from_north = shifted(widened[-1:], "space", GX)
    from_south = shifted(widened[:1], "space", -GX)
    return jnp.concatenate([from_north, widened, from_south], axis=0)


def group_act(field, gain, shift, count):
    width = field.shape[-1] // GROUPS
    grouped = field.reshape(-1, GROUPS, width)
    total = lax.psum(jnp.sum(grouped, axis=(0, 2)), ("tm", "space"))
    mean = total / count
    centered = grouped - mean[None, :, None]
    squares = lax.psum(jnp.sum(centered * centered, axis=(0, 2)), ("tm", "space"))
    spread = squares / count
    normed = (centered * lax.rsqrt(spread + EPS)[None, :, None]).reshape(field.shape)
    return jax.nn.silu(normed * gain + shift).astype(jnp.bfloat16)


def apply_taps(stack, kernel, frames_out, rows, cols):
    width = kernel.shape[3]
    total = None
    for step_t in range(3):
        for step_y in range(3):
            for step_x in range(3):
                window = stack[
                    step_t : step_t + frames_out, step_y : step_y + rows, step_x : step_x + cols, :
                ]
                term = jnp.dot(
                    window.reshape(-1, width),
                    kernel[step_t, step_y, step_x],
                    preferred_element_type=jnp.float32,
                )
                total = term if total is None else total + term
    return total


def relay_frame(padded):
    return shifted(padded, "tm", 1)


def conv_near(act, kernel_cols, bias):
    rows, cols, channels = act.shape
    padded = spatial_halo(act)
    previous = relay_frame(padded)
    earlier = relay_frame(previous)
    stack = jnp.stack([earlier, previous, padded])
    kernel_full = lax.all_gather(kernel_cols, "space", axis=3, tiled=True)
    total = apply_taps(stack, kernel_full, 1, rows, cols)
    return total.reshape(rows, cols, channels) + bias


def shards(
    latents,
    gain_first,
    shift_first,
    kernel_first,
    bias_first,
    gain_second,
    shift_second,
    kernel_second,
    bias_second,
):
    tile = latents[0, 0].astype(jnp.float32)
    rows, cols, channels = tile.shape
    count = float(lax.axis_size("tm") * lax.axis_size("space") * rows * cols * (channels // GROUPS))
    first_act = group_act(tile, gain_first, shift_first, count)
    cols_first, cols_second = (
        lax.all_gather(kernel_first, "tm", axis=4, tiled=True),
        lax.all_gather(kernel_second, "tm", axis=4, tiled=True),
    )
    first_out = conv_near(first_act, cols_first, bias_first)
    second_act = group_act(first_out, gain_second, shift_second, count)
    second_out = conv_near(second_act, cols_second, bias_second)
    return (tile + second_out).astype(jnp.bfloat16)[None, None]


def solution(mesh):
    placed = (
        P("tm", "space", None, None, None),
        P(),
        P(),
        P(None, None, None, "space", "tm"),
        P(),
        P(),
        P(),
        P(None, None, None, "space", "tm"),
        P(),
    )
    return jax.shard_map(
        shards,
        mesh=mesh,
        in_specs=placed,
        out_specs=P("tm", "space", None, None, None),
        check_vma=False,
    )
```

profile of v0, /device:TPU:62, one launch (start us, length us, event | category | flops | bytes accessed | tf_op | source)
XLA Modules:
  0.0 541.0 jit_solution(8671705609608427689)
XLA Ops:
  6.5 2.2 copy.14
  8.8 32.9 %all_gather.12 = bf16[3,3,3,6,384]{3,2,1,0,4:T(4,128)(2,1)S(1)} all-gather(bf16[3,3,3,6,96]{3,2,1,0,4:T(4,128)(2,1)} %copy.14), channel_id=1, replica_groups=mesh['tm'=4,'space'=64] {'tm'}, dimensions={4}, use_global_device_ids=true | all-gather | bytes 155520 | tf_op jit(solution)/shard_map/all_gather | solution.py:90
  41.7 4.8 copy.15
  46.5 2.2 copy.43
  48.8 32.0 %all_gather.14 = bf16[3,3,3,6,384]{3,2,1,0,4:T(4,128)(2,1)S(1)} all-gather(bf16[3,3,3,6,96]{3,2,1,0,4:T(4,128)(2,1)} %copy.43), channel_id=1, replica_groups=mesh['tm'=4,'space'=64] {'tm'}, dimensions={4}, use_global_device_ids=true | all-gather | bytes 155520 | tf_op jit(solution)/shard_map/all_gather | solution.py:91
  80.8 4.8 copy.44
  85.6 1.0 convert_reduce_fusion
  86.9 75.1 %psum.28 = f32[32]{0:T(128)S(1)} all-reduce(f32[32]{0:T(128)S(1)} %reduce_sum.51), channel_id=1, replica_groups=mesh['tm'=4,'space'=64] {'tm','space'}, use_global_device_ids=true, to_apply=%region_2.0 | all-reduce | flops 32 | bytes 256 | tf_op jit(solution)/shard_map/psum | solution.py:32
  162.2 1.0 fusion.35
  163.4 75.1 %psum.29 = f32[32]{0:T(128)S(1)} all-reduce(f32[32]{0:T(128)S(1)} %reduce_sum.54), channel_id=1, replica_groups=mesh['tm'=4,'space'=64] {'tm','space'}, use_global_device_ids=true, to_apply=%region_5.6 | all-reduce | flops 32 | bytes 256 | tf_op jit(solution)/shard_map/psum | solution.py:35
  238.8 1.1 fusion.46
  239.9 2.5 collective-permute-start
  242.4 3.1 collective-permute-start.1
  245.6 1.3 collective-permute-done.1
  246.9 3.7 collective-permute-start.2
  250.6 2.5 collective-permute-start.3
  253.2 3.3 collective-permute-done.3
  256.6 1.3 collective-permute-start.4
  258.0 8.4 %collective-permute-done.4 = bf16[10,42,384]{2,1,0:T(8,128)(2,1)S(1)} collective-permute-done((bf16[10,42,384]{2,1,0:T(8,128)(2,1)S(1)}, bf16[10,42,384]{2,1,0:T(8,128)(2,1)S(1)}, u32[]{:S(2)}, u32[]{:S(2)}) %collective-permute-start.4) | collective-permute-done | bytes 322592 | tf_op jit(solution)/shard_map/ppermute | solution.py:14
  266.4 1.3 collective-permute-start.5
  268.0 1.4 fusion.92
  269.5 7.9 %collective-permute-done.5 = bf16[10,42,384]{2,1,0:T(8,128)(2,1)S(1)} collective-permute-done((bf16[10,42,384]{2,1,0:T(8,128)(2,1)S(1)}, bf16[10,42,384]{2,1,0:T(8,128)(2,1)S(1)}, u32[]{:S(2)}, u32[]{:S(2)}) %collective-permute-start.5) | collective-permute-done | bytes 322592 | tf_op jit(solution)/shard_map/ppermute | solution.py:14
  277.4 1.1 fusion.91
  278.6 16.8 %fusion.85 = (bf16[1,1,1,384,384]{4,2,1,0,3:T(2,128)(2,1)S(1)}, bf16[1,1,1,384,384]{4,2,1,0,3:T(2,128)(2,1)S(1)}, bf16[1,1,1,384,384]{4,2,1,0,3:T(2,128)(2,1)S(1...) fusion(bf16[3,3,3,384,384]{4,2,1,0,3:T(4,128)(2,1)} %all-gather, ...), kind=kLoop, calls=%fused_computation.180 | loop fusion | bytes 11206656 | tf_op jit(solution)/shard_map/slice | solution.py:52
  299.2 7.0 %fusion.86 = (bf16[1,1,1,384,384]{4,2,1,0,3:T(2,128)(2,1)S(1)}, bf16[1,1,1,384,384]{4,2,1,0,3:T(2,128)(2,1)S(1)}, bf16[1,1,1,384,384]{4,2,1,0,3:T(2,128)(2,1)S(1...) fusion(bf16[3,3,3,384,384]{4,2,1,0,3:T(4,128)(2,1)} %all-gather, ...), kind=kLoop, calls=%fused_computation.181 | loop fusion | bytes 4718592 | tf_op jit(solution)/shard_map/slice | solution.py:52
  307.6 0.3 fusion.80
  308.6 0.8 fusion.27
  309.4 0.3 convolution_add_fusion.16
  311.8 0.4 add_reduce_fusion
  312.4 77.7 %psum.30 = f32[32]{0:T(128)S(1)} all-reduce(f32[32]{0:T(128)S(1)} %reduce_sum.72), channel_id=1, replica_groups=mesh['tm'=4,'space'=64] {'tm','space'}, use_global_device_ids=true, to_apply=%region_8.9 | all-reduce | flops 32 | bytes 256 | tf_op jit(solution)/shard_map/psum | solution.py:32
  390.5 72.8 %psum.31 = f32[32]{0:T(128)S(1)} all-reduce(f32[32]{0:T(128)S(1)} %reduce_sum.75), channel_id=1, replica_groups=mesh['tm'=4,'space'=64] {'tm','space'}, use_global_device_ids=true, to_apply=%region_11.12 | all-reduce | flops 32 | bytes 256 | tf_op jit(solution)/shard_map/psum | solution.py:35
  463.7 2.0 collective-permute-start.6
  465.7 3.6 collective-permute-start.7
  469.3 16.3 %fusion.83 = (bf16[1,1,1,384,384]{4,2,1,0,3:T(2,128)(2,1)S(1)}, bf16[1,1,1,384,384]{4,2,1,0,3:T(2,128)(2,1)S(1)}, bf16[1,1,1,384,384]{4,2,1,0,3:T(2,128)(2,1)S(1...) fusion(bf16[3,3,3,384,384]{4,2,1,0,3:T(4,128)(2,1)} %all-gather, ...), kind=kLoop, calls=%fused_computation.178 | loop fusion | bytes 11206656 | tf_op jit(solution)/shard_map/slice | solution.py:52
  485.8 1.9 collective-permute-start.8
  487.7 3.9 collective-permute-start.9
  491.6 6.9 %fusion.84 = (bf16[1,1,1,384,384]{4,2,1,0,3:T(2,128)(2,1)S(1)}, bf16[1,1,1,384,384]{4,2,1,0,3:T(2,128)(2,1)S(1)}, bf16[1,1,1,384,384]{4,2,1,0,3:T(2,128)(2,1)S(1...) fusion(bf16[3,3,3,384,384]{4,2,1,0,3:T(4,128)(2,1)} %all-gather, ...), kind=kLoop, calls=%fused_computation.179 | loop fusion | bytes 4718592 | tf_op jit(solution)/shard_map/slice | solution.py:52
  498.7 1.3 collective-permute-start.10
  500.7 11.3 %collective-permute-done.10 = bf16[10,42,384]{2,1,0:T(8,128)(2,1)S(1)} collective-permute-done((bf16[10,42,384]{2,1,0:T(8,128)(2,1)S(1)}, bf16[10,42,384]{2,1,0:T(8,128)(2,1)S(1)}, u32[]{:S(2)}, u32[]{:S(2)}) %collective-permute-start.10) | collective-permute-done | bytes 322592 | tf_op jit(solution)/shard_map/ppermute | solution.py:14
  512.9 0.3 fusion.54
  513.6 0.3 fusion.52
  514.3 0.3 fusion.50
  514.6 1.6 collective-permute-start.11
  516.5 0.3 fusion.48
  516.8 10.2 %collective-permute-done.11 = bf16[10,42,384]{2,1,0:T(8,128)(2,1)S(1)} collective-permute-done((bf16[10,42,384]{2,1,0:T(8,128)(2,1)S(1)}, bf16[10,42,384]{2,1,0:T(8,128)(2,1)S(1)}, u32[]{:S(2)}, u32[]{:S(2)}) %collective-permute-start.11) | collective-permute-done | bytes 322592 | tf_op jit(solution)/shard_map/ppermute | solution.py:14
  527.7 0.3 fusion.59
  530.1 0.7 fusion.33
  533.4 0.8 fusion.36
  (134 shorter events, 18.4 us)
Async XLA Ops:
  6.5 232.2 %copy-start.16 = (f32[384]{0:T(512)S(1)}, f32[384]{0:T(512)}, u32[]{:S(2)}) copy-start(f32[384]{0:T(512)} %param.10) | copy-start | bytes 4612
  6.5 232.2 %copy-start.15 = (f32[384]{0:T(512)S(1)}, f32[384]{0:T(512)}, u32[]{:S(2)}) copy-start(f32[384]{0:T(512)} %param.11) | copy-start | bytes 4612
  6.5 271.9 %all-gather.3.cloned.1.call-start = ((), (), s32[]{:S(2)}) async-start(), calls=%async_computation | async-start | bytes 10782720 | tf_op jit(solution)/shard_map/all_gather | solution.py:69
  46.5 422.8 %all-gather.5.cloned.1.call-start = ((), (), s32[]{:S(2)}) async-start(), calls=%async_computation.1 | async-start | bytes 10782720 | tf_op jit(solution)/shard_map/all_gather | solution.py:69
  239.9 5.6 %collective-permute-start = (bf16[8,1,384]{2,1,0:T(2,128)(2,1)S(1)}, bf16[8,1,384]{2,1,0:T(2,128)(2,1)S(1)}, u32[]{:S(2)}, u32[]{:S(2)}) collective-permute-start(bf16[8,1,384]{2,1,0:T(2,128)(2,1)S(1)} %get-tuple-element.119), channel_id=1, source_target_pairs={{0,1},{1,2},{2,3},{3,4},{4,5},{5,6},{6,7},{7,8},{8,9},{9,10},{10,1... | collective-permute-start | bytes 18440 | tf_op jit(solution)/shard_map/ppermute | solution.py:14
  242.4 4.5 collective-permute-start.1
  246.9 6.2 %collective-permute-start.2 = (bf16[1,42,384]{2,1,0:T(8,128)(2,1)S(1)}, bf16[1,42,384]{2,1,0:T(8,128)(2,1)S(1)}, u32[]{:S(2)}, u32[]{:S(2)}) collective-permute-start(bf16[1,42,384]{2,1,0:T(8,128)(2,1)S(1)} %get-tuple-element.115), channel_id=1, source_target_pairs={{0,8},{1,9},{2,10},{3,11},{4,12},{5,13},{6,14},{7,15},{8,16},{9,17... | collective-permute-start | bytes 96776 | tf_op jit(solution)/shard_map/ppermute | solution.py:14
  250.6 5.9 %collective-permute-start.3 = (bf16[1,42,384]{2,1,0:T(8,128)(2,1)S(1)}, bf16[1,42,384]{2,1,0:T(8,128)(2,1)S(1)}, u32[]{:S(2)}, u32[]{:S(2)}) collective-permute-start(bf16[1,42,384]{2,1,0:T(8,128)(2,1)S(1)} %get-tuple-element.116), channel_id=1, source_target_pairs={{8,0},{9,1},{10,2},{11,3},{12,4},{13,5},{14,6},{15,7},{16,8},{17,9... | collective-permute-start | bytes 96776 | tf_op jit(solution)/shard_map/ppermute | solution.py:14
  256.6 9.8 %collective-permute-start.4 = (bf16[10,42,384]{2,1,0:T(8,128)(2,1)S(1)}, bf16[10,42,384]{2,1,0:T(8,128)(2,1)S(1)}, u32[]{:S(2)}, u32[]{:S(2)}) collective-permute-start(bf16[10,42,384]{2,1,0:T(8,128)(2,1)S(1)} %pad_maximum_fusion), channel_id=1, source_target_pairs={{0,64},{64,128},{128,192},{1,65},{65,129},{129,193},{2,66},{66,130... | collective-permute-start | bytes 967688 | tf_op jit(solution)/shard_map/ppermute | solution.py:14
  266.4 10.9 %collective-permute-start.5 = (bf16[10,42,384]{2,1,0:T(8,128)(2,1)S(1)}, bf16[10,42,384]{2,1,0:T(8,128)(2,1)S(1)}, u32[]{:S(2)}, u32[]{:S(2)}) collective-permute-start(bf16[10,42,384]{2,1,0:T(8,128)(2,1)S(1)} %collective-permute-done.4), channel_id=1, source_target_pairs={{0,64},{64,128},{128,192},{1,65},{65,129},{129,193},{2,66},{66,130... | collective-permute-start | bytes 967688 | tf_op jit(solution)/shard_map/ppermute | solution.py:14
  278.5 16.9 %copy-start.13 = (bf16[1,8,40,384]{3,2,1,0:T(8,128)(2,1)S(1)}, bf16[1,8,40,384]{3,2,1,0:T(8,128)(2,1)}, u32[]{:S(2)}) copy-start(bf16[1,8,40,384]{3,2,1,0:T(8,128)(2,1)} %get-tuple-element.96) | copy-start | bytes 737284
  278.5 17.3 %copy-start.12 = (bf16[1,8,40,384]{3,2,1,0:T(8,128)(2,1)S(1)}, bf16[1,8,40,384]{3,2,1,0:T(8,128)(2,1)}, u32[]{:S(2)}) copy-start(bf16[1,8,40,384]{3,2,1,0:T(8,128)(2,1)} %get-tuple-element.105) | copy-start | bytes 737284
  278.5 17.6 %copy-start.11 = (bf16[1,8,40,384]{3,2,1,0:T(8,128)(2,1)S(1)}, bf16[1,8,40,384]{3,2,1,0:T(8,128)(2,1)}, u32[]{:S(2)}) copy-start(bf16[1,8,40,384]{3,2,1,0:T(8,128)(2,1)} %get-tuple-element.106) | copy-start | bytes 737284
  278.5 17.9 %copy-start.10 = (bf16[1,8,40,384]{3,2,1,0:T(8,128)(2,1)S(1)}, bf16[1,8,40,384]{3,2,1,0:T(8,128)(2,1)}, u32[]{:S(2)}) copy-start(bf16[1,8,40,384]{3,2,1,0:T(8,128)(2,1)} %get-tuple-element.107) | copy-start | bytes 737284
  278.5 18.3 %copy-start.9 = (bf16[1,8,40,384]{3,2,1,0:T(8,128)(2,1)S(1)}, bf16[1,8,40,384]{3,2,1,0:T(8,128)(2,1)}, u32[]{:S(2)}) copy-start(bf16[1,8,40,384]{3,2,1,0:T(8,128)(2,1)} %get-tuple-element.108) | copy-start | bytes 737284
  278.5 18.6 %copy-start.8 = (bf16[1,8,40,384]{3,2,1,0:T(8,128)(2,1)S(1)}, bf16[1,8,40,384]{3,2,1,0:T(8,128)(2,1)}, u32[]{:S(2)}) copy-start(bf16[1,8,40,384]{3,2,1,0:T(8,128)(2,1)} %get-tuple-element.109) | copy-start | bytes 737284
  278.5 18.9 %copy-start.7 = (bf16[1,8,40,384]{3,2,1,0:T(8,128)(2,1)S(1)}, bf16[1,8,40,384]{3,2,1,0:T(8,128)(2,1)}, u32[]{:S(2)}) copy-start(bf16[1,8,40,384]{3,2,1,0:T(8,128)(2,1)} %get-tuple-element.110) | copy-start | bytes 737284
  278.5 19.3 %copy-start.6 = (bf16[1,8,40,384]{3,2,1,0:T(8,128)(2,1)S(1)}, bf16[1,8,40,384]{3,2,1,0:T(8,128)(2,1)}, u32[]{:S(2)}) copy-start(bf16[1,8,40,384]{3,2,1,0:T(8,128)(2,1)} %get-tuple-element.111) | copy-start | bytes 737284
  278.5 19.6 %copy-start.5 = (bf16[1,8,40,384]{3,2,1,0:T(8,128)(2,1)S(1)}, bf16[1,8,40,384]{3,2,1,0:T(8,128)(2,1)}, u32[]{:S(2)}) copy-start(bf16[1,8,40,384]{3,2,1,0:T(8,128)(2,1)} %get-tuple-element.112) | copy-start | bytes 737284
  278.6 20.0 %copy-start.4 = (bf16[1,8,40,384]{3,2,1,0:T(8,128)(2,1)S(1)}, bf16[1,8,40,384]{3,2,1,0:T(8,128)(2,1)}, u32[]{:S(2)}) copy-start(bf16[1,8,40,384]{3,2,1,0:T(8,128)(2,1)} %get-tuple-element.104) | copy-start | bytes 737284
  295.4 10.8 %copy-start.3 = (bf16[1,8,40,384]{3,2,1,0:T(8,128)(2,1)S(1)}, bf16[1,8,40,384]{3,2,1,0:T(8,128)(2,1)}, u32[]{:S(2)}) copy-start(bf16[1,8,40,384]{3,2,1,0:T(8,128)(2,1)} %get-tuple-element.97) | copy-start | bytes 737284
  295.7 10.8 %copy-start.2 = (bf16[1,8,40,384]{3,2,1,0:T(8,128)(2,1)S(1)}, bf16[1,8,40,384]{3,2,1,0:T(8,128)(2,1)}, u32[]{:S(2)}) copy-start(bf16[1,8,40,384]{3,2,1,0:T(8,128)(2,1)} %get-tuple-element.98) | copy-start | bytes 737284
  296.1 10.8 %copy-start.1 = (bf16[1,8,40,384]{3,2,1,0:T(8,128)(2,1)S(1)}, bf16[1,8,40,384]{3,2,1,0:T(8,128)(2,1)}, u32[]{:S(2)}) copy-start(bf16[1,8,40,384]{3,2,1,0:T(8,128)(2,1)} %get-tuple-element.99) | copy-start | bytes 737284
  308.3 3.5 copy-start.14
  308.6 154.9 %copy-start.17 = (f32[384]{0:T(512)S(1)}, f32[384]{0:T(512)}, u32[]{:S(2)}) copy-start(f32[384]{0:T(512)} %param.15) | copy-start | bytes 4612
  308.6 154.9 %copy-start.18 = (f32[384]{0:T(512)S(1)}, f32[384]{0:T(512)}, u32[]{:S(2)}) copy-start(f32[384]{0:T(512)} %param.14) | copy-start | bytes 4612
  463.7 21.9 %collective-permute-start.6 = (bf16[8,1,384]{2,1,0:T(2,128)(2,1)S(1)}, bf16[8,1,384]{2,1,0:T(2,128)(2,1)S(1)}, u32[]{:S(2)}, u32[]{:S(2)}) collective-permute-start(bf16[8,1,384]{2,1,0:T(2,128)(2,1)S(1)} %get-tuple-element.117), channel_id=1, source_target_pairs={{0,1},{1,2},{2,3},{3,4},{4,5},{5,6},{6,7},{7,8},{8,9},{9,10},{10,1... | collective-permute-start | bytes 18440 | tf_op jit(solution)/shard_map/ppermute | solution.py:14
  465.7 20.0 %collective-permute-start.7 = (bf16[8,1,384]{2,1,0:T(2,128)(2,1)S(1)}, bf16[8,1,384]{2,1,0:T(2,128)(2,1)S(1)}, u32[]{:S(2)}, u32[]{:S(2)}) collective-permute-start(bf16[8,1,384]{2,1,0:T(2,128)(2,1)S(1)} %get-tuple-element.118), channel_id=1, source_target_pairs={{1,0},{2,1},{3,2},{4,3},{5,4},{6,5},{7,6},{8,7},{9,8},{10,9},{11,1... | collective-permute-start | bytes 18440 | tf_op jit(solution)/shard_map/ppermute | solution.py:14
  485.8 12.8 %collective-permute-start.8 = (bf16[1,42,384]{2,1,0:T(8,128)(2,1)S(1)}, bf16[1,42,384]{2,1,0:T(8,128)(2,1)S(1)}, u32[]{:S(2)}, u32[]{:S(2)}) collective-permute-start(bf16[1,42,384]{2,1,0:T(8,128)(2,1)S(1)} %get-tuple-element.113), channel_id=1, source_target_pairs={{0,8},{1,9},{2,10},{3,11},{4,12},{5,13},{6,14},{7,15},{8,16},{9,17... | collective-permute-start | bytes 96776 | tf_op jit(solution)/shard_map/ppermute | solution.py:14
  487.7 10.9 %collective-permute-start.9 = (bf16[1,42,384]{2,1,0:T(8,128)(2,1)S(1)}, bf16[1,42,384]{2,1,0:T(8,128)(2,1)S(1)}, u32[]{:S(2)}, u32[]{:S(2)}) collective-permute-start(bf16[1,42,384]{2,1,0:T(8,128)(2,1)S(1)} %get-tuple-element.114), channel_id=1, source_target_pairs={{8,0},{9,1},{10,2},{11,3},{12,4},{13,5},{14,6},{15,7},{16,8},{17,9... | collective-permute-start | bytes 96776 | tf_op jit(solution)/shard_map/ppermute | solution.py:14
  498.7 13.3 %collective-permute-start.10 = (bf16[10,42,384]{2,1,0:T(8,128)(2,1)S(1)}, bf16[10,42,384]{2,1,0:T(8,128)(2,1)S(1)}, u32[]{:S(2)}, u32[]{:S(2)}) collective-permute-start(bf16[10,42,384]{2,1,0:T(8,128)(2,1)S(1)} %pad_maximum_fusion.1), channel_id=1, source_target_pairs={{0,64},{64,128},{128,192},{1,65},{65,129},{129,193},{2,66},{66,130... | collective-permute-start | bytes 967688 | tf_op jit(solution)/shard_map/ppermute | solution.py:14
  514.6 12.4 %collective-permute-start.11 = (bf16[10,42,384]{2,1,0:T(8,128)(2,1)S(1)}, bf16[10,42,384]{2,1,0:T(8,128)(2,1)S(1)}, u32[]{:S(2)}, u32[]{:S(2)}) collective-permute-start(bf16[10,42,384]{2,1,0:T(8,128)(2,1)S(1)} %collective-permute-done.10), channel_id=1, source_target_pairs={{0,64},{64,128},{128,192},{1,65},{65,129},{129,193},{2,66},{66,130... | collective-permute-start | bytes 967688 | tf_op jit(solution)/shard_map/ppermute | solution.py:14
  530.0 3.4 copy-start
  530.0 3.4 copy-start.19
Sparse Core Ops, SparseCore 0:
  46.6 86.8 all-gather.2
  136.2 83.6 all-gather.4
where the time goes:
time: 542 us; the launch traced here: 541 us
  blocking collectives  366 us (68%)
  local copies, waits for them, and re-layouts  66 us (12%)
  waiting for transfers between devices  42.5 us (8%)
  starting transfers between devices  28.6 us (5%)
  matrix products  18.7 us (3%)
  between operations  14.3 us (3%)
    psum x2, blocking collectives, group_act(): total = lax.psum(jnp.sum(grouped, axis=(0, 2)), ('tm', 'space'))  153 us
    psum x2, blocking collectives, group_act(): lax.psum(jnp.sum(centered * centered, axis=(0, 2)), ('tm', 'space'))  148 us
    slice x4, local copies, waits for them, and re-layouts, apply_taps(): kernel[step_t, step_y, step_x]  47.1 us
    ppermute x12, waiting for transfers between devices, shifted(): lax.ppermute(value, axis, [(source, source + steps) for source in range(i...  42.5 us
    all_gather x1, blocking collectives, shards(): lax.all_gather(kernel_first, 'tm', axis=4, tiled=True)  32.9 us
    all_gather x1, blocking collectives, shards(): lax.all_gather(kernel_second, 'tm', axis=4, tiled=True)  32 us
    ppermute x12, starting transfers between devices, shifted(): lax.ppermute(value, axis, [(source, source + steps) for source in range(i...  28.6 us
    dot_general x54, matrix products, apply_taps(): jnp.dot(window.reshape(-1, width), kernel[step_t, step_y, step_x], prefer...  18.7 us
  transfers between devices with their start and end apart: 14, of which 6 were waited for; matrix products, arithmetic and copies ran while one was open for 14% of the time, Pallas kernels for 0%

commit v1 on v0

--- a/solution.py
+++ b/solution.py
@@ -88,7 +88,9 @@
     first_act = group_act(tile, gain_first, shift_first, count)
     cols_first, cols_second = (
         lax.all_gather(kernel_first, "tm", axis=4, tiled=True),
-        lax.all_gather(kernel_second, "tm", axis=4, tiled=True),
+        jnp.concatenate(
+            lax.all_to_all(jnp.stack([kernel_second] * lax.axis_size("tm")), "tm", 0, 0), axis=4
+        ),
     )
     first_out = conv_near(first_act, cols_first, bias_first)
     second_act = group_act(first_out, gain_second, shift_second, count)

time: 542 us -> 512 us (0.945)
  blocking collectives: 366 us -> 344 us
  waiting for transfers between devices: 42.5 us -> 35.3 us
    all_gather x1 -> x0, blocking collectives: 32 us -> none  [shards(): lax.all_gather(kernel_second, 'tm', axis=4, tiled=True)]
    all_to_all x0 -> x1, blocking collectives: none -> 8.7 us  [shards(): lax.all_to_all(jnp.stack([kernel_second] * lax.axis_size('tm')), 'tm', 0, 0)]
    ppermute x12, waiting for transfers between devices: 42.5 us -> 35.2 us  [shifted(): lax.ppermute(value, axis, [(source, source + steps) for source in range(i...]
  transfers between devices with their start and end apart: 14 -> 14, of which waited for: 6 -> 7; matrix products, arithmetic and copies ran while one was open for 14% -> 13% of each run, Pallas kernels for 0% -> 0%
where the time goes in v1:
time: 512 us; the launch traced here: 506 us
  blocking collectives  344 us (67%)
  local copies, waits for them, and re-layouts  60.9 us (12%)
  waiting for transfers between devices  35.3 us (7%)
  starting transfers between devices  28.5 us (6%)
  matrix products  18.7 us (4%)
  between operations  14.3 us (3%)
  other arithmetic  5.27 us (1%)
    psum x2, blocking collectives, group_act(): total = lax.psum(jnp.sum(grouped, axis=(0, 2)), ('tm', 'space'))  154 us
    psum x2, blocking collectives, group_act(): lax.psum(jnp.sum(centered * centered, axis=(0, 2)), ('tm', 'space'))  148 us
    slice x4, local copies, waits for them, and re-layouts, apply_taps(): kernel[step_t, step_y, step_x]  47.2 us
    ppermute x12, waiting for transfers between devices, shifted(): lax.ppermute(value, axis, [(source, source + steps) for source in range(i...  35.2 us
    all_gather x1, blocking collectives, shards(): lax.all_gather(kernel_first, 'tm', axis=4, tiled=True)  32.9 us
    ppermute x12, starting transfers between devices, shifted(): lax.ppermute(value, axis, [(source, source + steps) for source in range(i...  28.5 us
    dot_general x54, matrix products, apply_taps(): jnp.dot(window.reshape(-1, width), kernel[step_t, step_y, step_x], prefer...  18.7 us
  transfers between devices with their start and end apart: 14, of which 7 were waited for; matrix products, arithmetic and copies ran while one was open for 13% of the time, Pallas kernels for 0%

profile of v1, /device:TPU:62, one launch (start us, length us, event | category | flops | bytes accessed | tf_op | source)
XLA Modules:
  0.0 506.5 jit_solution(5880331351095292506)
XLA Ops:
  6.5 2.2 copy.14
  8.8 32.9 %all_gather.9 = bf16[3,3,3,6,384]{3,2,1,0,4:T(4,128)(2,1)S(1)} all-gather(bf16[3,3,3,6,96]{3,2,1,0,4:T(4,128)(2,1)} %copy.14), channel_id=1, replica_groups=mesh['tm'=4,'space'=64] {'tm'}, dimensions={4}, use_global_device_ids=true | all-gather | bytes 155520 | tf_op jit(solution)/shard_map/all_gather | solution.py:90
  41.7 4.8 copy.15
  46.5 0.8 stack.29
  47.4 8.7 %all_to_all.5 = bf16[4,3,3,3,6,96]{5,4,3,2,1,0:T(8,128)(2,1)S(1)} all-to-all(bf16[4,3,3,3,6,96]{5,4,3,2,1,0:T(8,128)(2,1)S(1)} %stack.29), channel_id=1, replica_groups=mesh['tm'=4,'space'=64] {'tm'}, dimensions={0} | all-to-all | bytes 248832 | tf_op jit(solution)/shard_map/all_to_all | solution.py:92
  56.2 0.9 reshape.283
  57.1 1.0 convert_reduce_fusion
  58.4 76.2 %psum.28 = f32[32]{0:T(128)S(1)} all-reduce(f32[32]{0:T(128)S(1)} %reduce_sum.51), channel_id=1, replica_groups=mesh['tm'=4,'space'=64] {'tm','space'}, use_global_device_ids=true, to_apply=%region_2.0 | all-reduce | flops 32 | bytes 256 | tf_op jit(solution)/shard_map/psum | solution.py:32
  134.7 1.0 fusion.35
  136.0 74.7 %psum.29 = f32[32]{0:T(128)S(1)} all-reduce(f32[32]{0:T(128)S(1)} %reduce_sum.54), channel_id=1, replica_groups=mesh['tm'=4,'space'=64] {'tm','space'}, use_global_device_ids=true, to_apply=%region_5.6 | all-reduce | flops 32 | bytes 256 | tf_op jit(solution)/shard_map/psum | solution.py:35
  210.9 1.1 fusion.46
  212.1 1.9 collective-permute-start
  214.0 3.6 collective-permute-start.1
  217.7 1.3 collective-permute-done.1
  219.1 3.5 collective-permute-start.2
  222.6 2.4 collective-permute-start.3
  225.0 3.5 collective-permute-done.3
  228.6 1.3 collective-permute-start.4
  230.0 8.4 %collective-permute-done.4 = bf16[10,42,384]{2,1,0:T(8,128)(2,1)S(1)} collective-permute-done((bf16[10,42,384]{2,1,0:T(8,128)(2,1)S(1)}, bf16[10,42,384]{2,1,0:T(8,128)(2,1)S(1)}, u32[]{:S(2)}, u32[]{:S(2)}) %collective-permute-start.4) | collective-permute-done | bytes 322592 | tf_op jit(solution)/shard_map/ppermute | solution.py:14
  238.4 1.3 collective-permute-start.5
  239.9 1.4 fusion.92
  241.4 7.8 %collective-permute-done.5 = bf16[10,42,384]{2,1,0:T(8,128)(2,1)S(1)} collective-permute-done((bf16[10,42,384]{2,1,0:T(8,128)(2,1)S(1)}, bf16[10,42,384]{2,1,0:T(8,128)(2,1)S(1)}, u32[]{:S(2)}, u32[]{:S(2)}) %collective-permute-start.5) | collective-permute-done | bytes 322592 | tf_op jit(solution)/shard_map/ppermute | solution.py:14
  249.2 1.1 fusion.91
  250.4 16.8 %fusion.85 = (bf16[1,1,1,384,384]{4,2,1,0,3:T(2,128)(2,1)S(1)}, bf16[1,1,1,384,384]{4,2,1,0,3:T(2,128)(2,1)S(1)}, bf16[1,1,1,384,384]{4,2,1,0,3:T(2,128)(2,1)S(1...) fusion(bf16[3,3,3,384,384]{4,2,1,0,3:T(4,128)(2,1)} %all-gather, ...), kind=kLoop, calls=%fused_computation.180 | loop fusion | bytes 11206656 | tf_op jit(solution)/shard_map/slice | solution.py:52
  271.0 7.0 %fusion.86 = (bf16[1,1,1,384,384]{4,2,1,0,3:T(2,128)(2,1)S(1)}, bf16[1,1,1,384,384]{4,2,1,0,3:T(2,128)(2,1)S(1)}, bf16[1,1,1,384,384]{4,2,1,0,3:T(2,128)(2,1)S(1...) fusion(bf16[3,3,3,384,384]{4,2,1,0,3:T(4,128)(2,1)} %all-gather, ...), kind=kLoop, calls=%fused_computation.181 | loop fusion | bytes 4718592 | tf_op jit(solution)/shard_map/slice | solution.py:52
  279.4 0.3 fusion.80
  280.5 0.8 fusion.27
  281.3 0.3 convolution_add_fusion.16
  283.6 0.4 add_reduce_fusion
  284.2 77.9 %psum.30 = f32[32]{0:T(128)S(1)} all-reduce(f32[32]{0:T(128)S(1)} %reduce_sum.72), channel_id=1, replica_groups=mesh['tm'=4,'space'=64] {'tm','space'}, use_global_device_ids=true, to_apply=%region_8.9 | all-reduce | flops 32 | bytes 256 | tf_op jit(solution)/shard_map/psum | solution.py:32
  362.6 73.1 %psum.31 = f32[32]{0:T(128)S(1)} all-reduce(f32[32]{0:T(128)S(1)} %reduce_sum.75), channel_id=1, replica_groups=mesh['tm'=4,'space'=64] {'tm','space'}, use_global_device_ids=true, to_apply=%region_11.12 | all-reduce | flops 32 | bytes 256 | tf_op jit(solution)/shard_map/psum | solution.py:35
  436.1 1.9 collective-permute-start.6
  438.1 3.6 collective-permute-start.7
  441.8 1.4 collective-permute-done.7
  443.2 4.2 collective-permute-start.8
  447.4 1.9 collective-permute-start.9
  449.4 3.9 collective-permute-done.9
  453.4 1.3 collective-permute-start.10
  455.1 16.4 %fusion.83 = (bf16[1,1,1,384,384]{4,2,1,0,3:T(2,128)(2,1)S(1)}, bf16[1,1,1,384,384]{4,2,1,0,3:T(2,128)(2,1)S(1)}, bf16[1,1,1,384,384]{4,2,1,0,3:T(2,128)(2,1)S(1...) fusion(bf16[3,3,3,384,384]{4,2,1,0,3:T(4,128)(2,1)} %all-gather, ...), kind=kLoop, calls=%fused_computation.178 | loop fusion | bytes 11206656 | tf_op jit(solution)/shard_map/slice | solution.py:52
  471.5 7.0 %fusion.84 = (bf16[1,1,1,384,384]{4,2,1,0,3:T(2,128)(2,1)S(1)}, bf16[1,1,1,384,384]{4,2,1,0,3:T(2,128)(2,1)S(1)}, bf16[1,1,1,384,384]{4,2,1,0,3:T(2,128)(2,1)S(1...) fusion(bf16[3,3,3,384,384]{4,2,1,0,3:T(4,128)(2,1)} %all-gather, ...), kind=kLoop, calls=%fused_computation.179 | loop fusion | bytes 4718592 | tf_op jit(solution)/shard_map/slice | solution.py:52
  479.4 0.3 fusion.55
  480.1 0.3 fusion.53
  480.7 0.3 fusion.51
  481.4 1.6 collective-permute-start.11
  483.3 0.3 fusion.48
  483.6 8.9 %collective-permute-done.11 = bf16[10,42,384]{2,1,0:T(8,128)(2,1)S(1)} collective-permute-done((bf16[10,42,384]{2,1,0:T(8,128)(2,1)S(1)}, bf16[10,42,384]{2,1,0:T(8,128)(2,1)S(1)}, u32[]{:S(2)}, u32[]{:S(2)}) %collective-permute-start.11) | collective-permute-done | bytes 322592 | tf_op jit(solution)/shard_map/ppermute | solution.py:14
  495.5 0.7 fusion.33
  498.9 0.8 fusion.36
  (135 shorter events, 18.8 us)
Async XLA Ops:
  6.5 204.4 %copy-start.16 = (f32[384]{0:T(512)S(1)}, f32[384]{0:T(512)}, u32[]{:S(2)}) copy-start(f32[384]{0:T(512)} %param.10) | copy-start | bytes 4612
  6.5 204.4 %copy-start.15 = (f32[384]{0:T(512)S(1)}, f32[384]{0:T(512)}, u32[]{:S(2)}) copy-start(f32[384]{0:T(512)} %param.11) | copy-start | bytes 4612
  6.5 243.8 %all-gather.3.cloned.1.call-start = ((), (), s32[]{:S(2)}) async-start(), calls=%async_computation.1 | async-start | bytes 10782720 | tf_op jit(solution)/shard_map/all_gather | solution.py:69
  46.5 408.6 %all-gather.5.cloned.1.call-start = ((), (), s32[]{:S(2)}) async-start(), calls=%async_computation.2 | async-start | bytes 10782720 | tf_op jit(solution)/shard_map/all_gather | solution.py:69
  212.1 5.6 %collective-permute-start = (bf16[8,1,384]{2,1,0:T(2,128)(2,1)S(1)}, bf16[8,1,384]{2,1,0:T(2,128)(2,1)S(1)}, u32[]{:S(2)}, u32[]{:S(2)}) collective-permute-start(bf16[8,1,384]{2,1,0:T(2,128)(2,1)S(1)} %get-tuple-element.119), channel_id=1, source_target_pairs={{0,1},{1,2},{2,3},{3,4},{4,5},{5,6},{6,7},{7,8},{8,9},{9,10},{10,1... | collective-permute-start | bytes 18440 | tf_op jit(solution)/shard_map/ppermute | solution.py:14
  214.0 5.0 collective-permute-start.1
  219.1 5.9 %collective-permute-start.2 = (bf16[1,42,384]{2,1,0:T(8,128)(2,1)S(1)}, bf16[1,42,384]{2,1,0:T(8,128)(2,1)S(1)}, u32[]{:S(2)}, u32[]{:S(2)}) collective-permute-start(bf16[1,42,384]{2,1,0:T(8,128)(2,1)S(1)} %get-tuple-element.115), channel_id=1, source_target_pairs={{0,8},{1,9},{2,10},{3,11},{4,12},{5,13},{6,14},{7,15},{8,16},{9,17... | collective-permute-start | bytes 96776 | tf_op jit(solution)/shard_map/ppermute | solution.py:14
  222.6 5.9 %collective-permute-start.3 = (bf16[1,42,384]{2,1,0:T(8,128)(2,1)S(1)}, bf16[1,42,384]{2,1,0:T(8,128)(2,1)S(1)}, u32[]{:S(2)}, u32[]{:S(2)}) collective-permute-start(bf16[1,42,384]{2,1,0:T(8,128)(2,1)S(1)} %get-tuple-element.116), channel_id=1, source_target_pairs={{8,0},{9,1},{10,2},{11,3},{12,4},{13,5},{14,6},{15,7},{16,8},{17,9... | collective-permute-start | bytes 96776 | tf_op jit(solution)/shard_map/ppermute | solution.py:14
  228.6 9.8 %collective-permute-start.4 = (bf16[10,42,384]{2,1,0:T(8,128)(2,1)S(1)}, bf16[10,42,384]{2,1,0:T(8,128)(2,1)S(1)}, u32[]{:S(2)}, u32[]{:S(2)}) collective-permute-start(bf16[10,42,384]{2,1,0:T(8,128)(2,1)S(1)} %pad_maximum_fusion), channel_id=1, source_target_pairs={{0,64},{64,128},{128,192},{1,65},{65,129},{129,193},{2,66},{66,130... | collective-permute-start | bytes 967688 | tf_op jit(solution)/shard_map/ppermute | solution.py:14
  238.4 10.8 %collective-permute-start.5 = (bf16[10,42,384]{2,1,0:T(8,128)(2,1)S(1)}, bf16[10,42,384]{2,1,0:T(8,128)(2,1)S(1)}, u32[]{:S(2)}, u32[]{:S(2)}) collective-permute-start(bf16[10,42,384]{2,1,0:T(8,128)(2,1)S(1)} %collective-permute-done.4), channel_id=1, source_target_pairs={{0,64},{64,128},{128,192},{1,65},{65,129},{129,193},{2,66},{66,130... | collective-permute-start | bytes 967688 | tf_op jit(solution)/shard_map/ppermute | solution.py:14
  250.3 16.9 %copy-start.13 = (bf16[1,8,40,384]{3,2,1,0:T(8,128)(2,1)S(1)}, bf16[1,8,40,384]{3,2,1,0:T(8,128)(2,1)}, u32[]{:S(2)}) copy-start(bf16[1,8,40,384]{3,2,1,0:T(8,128)(2,1)} %get-tuple-element.96) | copy-start | bytes 737284
  250.3 17.3 %copy-start.12 = (bf16[1,8,40,384]{3,2,1,0:T(8,128)(2,1)S(1)}, bf16[1,8,40,384]{3,2,1,0:T(8,128)(2,1)}, u32[]{:S(2)}) copy-start(bf16[1,8,40,384]{3,2,1,0:T(8,128)(2,1)} %get-tuple-element.105) | copy-start | bytes 737284
  250.3 17.6 %copy-start.11 = (bf16[1,8,40,384]{3,2,1,0:T(8,128)(2,1)S(1)}, bf16[1,8,40,384]{3,2,1,0:T(8,128)(2,1)}, u32[]{:S(2)}) copy-start(bf16[1,8,40,384]{3,2,1,0:T(8,128)(2,1)} %get-tuple-element.106) | copy-start | bytes 737284
  250.3 17.9 %copy-start.10 = (bf16[1,8,40,384]{3,2,1,0:T(8,128)(2,1)S(1)}, bf16[1,8,40,384]{3,2,1,0:T(8,128)(2,1)}, u32[]{:S(2)}) copy-start(bf16[1,8,40,384]{3,2,1,0:T(8,128)(2,1)} %get-tuple-element.107) | copy-start | bytes 737284
  250.3 18.3 %copy-start.9 = (bf16[1,8,40,384]{3,2,1,0:T(8,128)(2,1)S(1)}, bf16[1,8,40,384]{3,2,1,0:T(8,128)(2,1)}, u32[]{:S(2)}) copy-start(bf16[1,8,40,384]{3,2,1,0:T(8,128)(2,1)} %get-tuple-element.108) | copy-start | bytes 737284
  250.4 18.6 %copy-start.8 = (bf16[1,8,40,384]{3,2,1,0:T(8,128)(2,1)S(1)}, bf16[1,8,40,384]{3,2,1,0:T(8,128)(2,1)}, u32[]{:S(2)}) copy-start(bf16[1,8,40,384]{3,2,1,0:T(8,128)(2,1)} %get-tuple-element.109) | copy-start | bytes 737284
  250.4 19.0 %copy-start.7 = (bf16[1,8,40,384]{3,2,1,0:T(8,128)(2,1)S(1)}, bf16[1,8,40,384]{3,2,1,0:T(8,128)(2,1)}, u32[]{:S(2)}) copy-start(bf16[1,8,40,384]{3,2,1,0:T(8,128)(2,1)} %get-tuple-element.110) | copy-start | bytes 737284
  250.4 19.3 %copy-start.6 = (bf16[1,8,40,384]{3,2,1,0:T(8,128)(2,1)S(1)}, bf16[1,8,40,384]{3,2,1,0:T(8,128)(2,1)}, u32[]{:S(2)}) copy-start(bf16[1,8,40,384]{3,2,1,0:T(8,128)(2,1)} %get-tuple-element.111) | copy-start | bytes 737284
  250.4 19.6 %copy-start.5 = (bf16[1,8,40,384]{3,2,1,0:T(8,128)(2,1)S(1)}, bf16[1,8,40,384]{3,2,1,0:T(8,128)(2,1)}, u32[]{:S(2)}) copy-start(bf16[1,8,40,384]{3,2,1,0:T(8,128)(2,1)} %get-tuple-element.112) | copy-start | bytes 737284
  250.4 20.0 %copy-start.4 = (bf16[1,8,40,384]{3,2,1,0:T(8,128)(2,1)S(1)}, bf16[1,8,40,384]{3,2,1,0:T(8,128)(2,1)}, u32[]{:S(2)}) copy-start(bf16[1,8,40,384]{3,2,1,0:T(8,128)(2,1)} %get-tuple-element.104) | copy-start | bytes 737284
  267.2 10.9 %copy-start.3 = (bf16[1,8,40,384]{3,2,1,0:T(8,128)(2,1)S(1)}, bf16[1,8,40,384]{3,2,1,0:T(8,128)(2,1)}, u32[]{:S(2)}) copy-start(bf16[1,8,40,384]{3,2,1,0:T(8,128)(2,1)} %get-tuple-element.97) | copy-start | bytes 737284
  267.6 10.8 %copy-start.2 = (bf16[1,8,40,384]{3,2,1,0:T(8,128)(2,1)S(1)}, bf16[1,8,40,384]{3,2,1,0:T(8,128)(2,1)}, u32[]{:S(2)}) copy-start(bf16[1,8,40,384]{3,2,1,0:T(8,128)(2,1)} %get-tuple-element.98) | copy-start | bytes 737284
  267.9 10.8 %copy-start.1 = (bf16[1,8,40,384]{3,2,1,0:T(8,128)(2,1)S(1)}, bf16[1,8,40,384]{3,2,1,0:T(8,128)(2,1)}, u32[]{:S(2)}) copy-start(bf16[1,8,40,384]{3,2,1,0:T(8,128)(2,1)} %get-tuple-element.99) | copy-start | bytes 737284
  280.1 3.5 copy-start.14
  280.5 155.4 %copy-start.17 = (f32[384]{0:T(512)S(1)}, f32[384]{0:T(512)}, u32[]{:S(2)}) copy-start(f32[384]{0:T(512)} %param.15) | copy-start | bytes 4612
  280.5 155.4 %copy-start.18 = (f32[384]{0:T(512)S(1)}, f32[384]{0:T(512)}, u32[]{:S(2)}) copy-start(f32[384]{0:T(512)} %param.14) | copy-start | bytes 4612
  436.1 5.6 %collective-permute-start.6 = (bf16[8,1,384]{2,1,0:T(2,128)(2,1)S(1)}, bf16[8,1,384]{2,1,0:T(2,128)(2,1)S(1)}, u32[]{:S(2)}, u32[]{:S(2)}) collective-permute-start(bf16[8,1,384]{2,1,0:T(2,128)(2,1)S(1)} %get-tuple-element.117), channel_id=1, source_target_pairs={{0,1},{1,2},{2,3},{3,4},{4,5},{5,6},{6,7},{7,8},{8,9},{9,10},{10,1... | collective-permute-start | bytes 18440 | tf_op jit(solution)/shard_map/ppermute | solution.py:14
  438.1 5.1 %collective-permute-start.7 = (bf16[8,1,384]{2,1,0:T(2,128)(2,1)S(1)}, bf16[8,1,384]{2,1,0:T(2,128)(2,1)S(1)}, u32[]{:S(2)}, u32[]{:S(2)}) collective-permute-start(bf16[8,1,384]{2,1,0:T(2,128)(2,1)S(1)} %get-tuple-element.118), channel_id=1, source_target_pairs={{1,0},{2,1},{3,2},{4,3},{5,4},{6,5},{7,6},{8,7},{9,8},{10,9},{11,1... | collective-permute-start | bytes 18440 | tf_op jit(solution)/shard_map/ppermute | solution.py:14
  443.2 6.1 %collective-permute-start.8 = (bf16[1,42,384]{2,1,0:T(8,128)(2,1)S(1)}, bf16[1,42,384]{2,1,0:T(8,128)(2,1)S(1)}, u32[]{:S(2)}, u32[]{:S(2)}) collective-permute-start(bf16[1,42,384]{2,1,0:T(8,128)(2,1)S(1)} %get-tuple-element.113), channel_id=1, source_target_pairs={{0,8},{1,9},{2,10},{3,11},{4,12},{5,13},{6,14},{7,15},{8,16},{9,17... | collective-permute-start | bytes 96776 | tf_op jit(solution)/shard_map/ppermute | solution.py:14
  447.4 5.9 %collective-permute-start.9 = (bf16[1,42,384]{2,1,0:T(8,128)(2,1)S(1)}, bf16[1,42,384]{2,1,0:T(8,128)(2,1)S(1)}, u32[]{:S(2)}, u32[]{:S(2)}) collective-permute-start(bf16[1,42,384]{2,1,0:T(8,128)(2,1)S(1)} %get-tuple-element.114), channel_id=1, source_target_pairs={{8,0},{9,1},{10,2},{11,3},{12,4},{13,5},{14,6},{15,7},{16,8},{17,9... | collective-permute-start | bytes 96776 | tf_op jit(solution)/shard_map/ppermute | solution.py:14
  453.4 25.4 %collective-permute-start.10 = (bf16[10,42,384]{2,1,0:T(8,128)(2,1)S(1)}, bf16[10,42,384]{2,1,0:T(8,128)(2,1)S(1)}, u32[]{:S(2)}, u32[]{:S(2)}) collective-permute-start(bf16[10,42,384]{2,1,0:T(8,128)(2,1)S(1)} %pad_maximum_fusion.1), channel_id=1, source_target_pairs={{0,64},{64,128},{128,192},{1,65},{65,129},{129,193},{2,66},{66,130... | collective-permute-start | bytes 967688 | tf_op jit(solution)/shard_map/ppermute | solution.py:14
  481.4 11.1 %collective-permute-start.11 = (bf16[10,42,384]{2,1,0:T(8,128)(2,1)S(1)}, bf16[10,42,384]{2,1,0:T(8,128)(2,1)S(1)}, u32[]{:S(2)}, u32[]{:S(2)}) collective-permute-start(bf16[10,42,384]{2,1,0:T(8,128)(2,1)S(1)} %collective-permute-done.10), channel_id=1, source_target_pairs={{0,64},{64,128},{128,192},{1,65},{65,129},{129,193},{2,66},{66,130... | collective-permute-start | bytes 967688 | tf_op jit(solution)/shard_map/ppermute | solution.py:14
  495.5 3.4 copy-start
  495.5 3.4 copy-start.19
Sparse Core Ops, SparseCore 0:
  46.6 86.4 all-gather.2
  135.8 83.7 all-gather.4
